TPU v7x, 256 devices: a whole 4x4x8 slice. The times are simulated.
256 devices in a mesh: gx: 8 (over y, core), gy: 8 (over z_hi, x), af: 4 (over z_lo).
Axes of the slice: x: 4, y: 4, z: 8 (z_hi: 2, z_lo: 4; z = z_hi * 4 + z_lo), core: 2. Of those that a mesh axis runs over, the one named last changes fastest.
Arguments:
- volume: bfloat16 [32, 32, 128, 128], P('af', 'gx', 'gy'), may hold values from -6 to 6
- weight_one: bfloat16 [32, 32, 3, 3, 3], P('af'), may hold values from -0.21875 to 0.21875
- bias_one: float32 [32], P('af'), may hold values from -1 to 1
- weight_two: bfloat16 [32, 32, 3, 3, 3], P('af'), may hold values from -0.21875 to 0.21875
- cotangent: bfloat16 [32, 32, 128, 128], P('af', 'gx', 'gy'), may hold values from -6 to 6
Outputs:
- output: bfloat16 [32, 32, 128, 128], P('af', 'gx', 'gy')
- input_grad: bfloat16 [32, 32, 128, 128], P('af', 'gx', 'gy')
- grad_one: float32 [32, 32, 3, 3, 3], P('af')
- bias_grad: float32 [32], P('af')
- grad_two: float32 [32, 32, 3, 3, 3], P('af')
All inputs are finite; a program needn't handle non-finite values.
Results may differ from a plain program's by a relative error of at most 0.0065.
Values may be sent and summed in bfloat16 or wider, within the bound.
A program may use at most 64 MiB of HBM per device.

v0:
```python
import math
import jax
import jax.numpy as jnp
from jax import lax
from jax.sharding import PartitionSpec as P


def with_halo(cells, sides, width):
    for axis, dim in sides:
        count = lax.axis_size(axis)
        ends = count - 1
        head = lax.slice_in_dim(cells, 0, width, axis=dim)
        tail = lax.slice_in_dim(cells, cells.shape[dim] - width, cells.shape[dim], axis=dim)
        cells = jnp.concatenate(
            [
                lax.ppermute(tail, axis, [(i, (i + 1) % count) for i in range(ends)]),
                cells,
                lax.ppermute(head, axis, [((i + 1) % count, i) for i in range(ends)]),
            ],
            axis=dim,
        )
    return cells


def conv_valid(padded, weight):
    size_x = padded.shape[1] - 2
    size_y = padded.shape[2] - 2
    size_z = padded.shape[3] - 2
    total = jnp.zeros((weight.shape[0], size_x, size_y, size_z), jnp.float32)
    for off_x in range(3):
        for off_y in range(3):
            for off_z in range(3):
                window = padded[
                    :, off_x : off_x + size_x, off_y : off_y + size_y, off_z : off_z + size_z
                ]
                total = total + jnp.einsum(
                    "oi,ixyz->oxyz",
                    weight[:, :, off_x, off_y, off_z],
                    window,
                    preferred_element_type=jnp.float32,
                )
    return total


def kernel_grad(padded, cot_field):
    size_x = cot_field.shape[1]
    size_y = cot_field.shape[2]
    size_z = cot_field.shape[3]
    blocks = []
    for off_x in range(3):
        for off_y in range(3):
            for off_z in range(3):
                window = padded[
                    :, off_x : off_x + size_x, off_y : off_y + size_y, off_z : off_z + size_z
                ]
                blocks.append(
                    jnp.einsum(
                        "oxyz,ixyz->oi", cot_field, window, preferred_element_type=jnp.float32
                    )
                )
    stacked = jnp.stack(blocks, axis=-1)
    return stacked.reshape(cot_field.shape[0], padded.shape[0], 3, 3, 3)


def flipped(weight):
    return jnp.transpose(jnp.flip(weight, (2, 3, 4)), (1, 0, 2, 3, 4))


def depth_pad(values):
    return jnp.pad(values, ((0, 0), (0, 0), (0, 0), (1, 1)))


def full_padded(values):
    gathered = lax.all_gather(values, "af", axis=0, tiled=True)
    rimmed = with_halo(gathered, (("gx", 1), ("gy", 2)), 1)
    return depth_pad(rimmed)


def silu_grad(hidden_grad, pre_act):
    sigma_vals = jax.nn.sigmoid(pre_act)
    return (hidden_grad * sigma_vals * (1.0 + pre_act * (1.0 - sigma_vals))).astype(jnp.bfloat16)


def body(volume, weight_one, bias_one, weight_two, cotangent):
    own_rows = volume.shape[0]
    vol_pad = full_padded(volume)
    pre_act = conv_valid(vol_pad, weight_one) + bias_one[:, None, None, None]
    hidden = jax.nn.silu(pre_act).astype(jnp.bfloat16)
    hid_pad = full_padded(hidden)
    output = conv_valid(hid_pad, weight_two).astype(jnp.bfloat16)
    local_two = kernel_grad(hid_pad, cotangent)
    every_one, every_two = (
        lax.all_gather(weight_one, "af", axis=0, tiled=True),
        lax.all_gather(weight_two, "af", axis=0, tiled=True),
    )
    first_row = lax.axis_index("af") * own_rows

    def transposed(cot_field, every_w):
        padded = full_padded(cot_field)
        turned = lax.dynamic_slice_in_dim(flipped(every_w), first_row, own_rows, 0)
        return conv_valid(padded, turned)

    hidden_grad = transposed(cotangent, every_two)
    pre_grad = silu_grad(hidden_grad, pre_act)
    local_one = kernel_grad(vol_pad, pre_grad)
    local_bias = jnp.sum(pre_grad, axis=(1, 2, 3), dtype=jnp.float32)
    input_grad = transposed(pre_grad, every_one).astype(jnp.bfloat16)
    summed_one, summed_bias, summed_two = lax.psum((local_one, local_bias, local_two), ("gx", "gy"))
    cell_total = (
        volume.shape[1]
        * lax.axis_size("gx")
        * volume.shape[2]
        * lax.axis_size("gy")
        * volume.shape[3]
    )
    grad_scale = 1.0 / math.sqrt(cell_total)
    return (
        output,
        input_grad,
        summed_one * grad_scale,
        summed_bias * grad_scale,
        summed_two * grad_scale,
    )


def solution(mesh):
    return jax.shard_map(
        body,
        mesh=mesh,
        in_specs=(
            P("af", "gx", "gy", None),
            P("af", None, None, None, None),
            P("af"),
            P("af", None, None, None, None),
            P("af", "gx", "gy", None),
        ),
        out_specs=(
            P("af", "gx", "gy", None),
            P("af", "gx", "gy", None),
            P("af", None, None, None, None),
            P("af"),
            P("af", None, None, None, None),
        ),
        check_vma=False,
    )
```

profile of v0, /device:TPU:0, one launch (start us, length us, event | category | flops | bytes accessed | tf_op | source)
XLA Modules:
  0.0 645.6 jit_solution(11498958030644135914)
XLA Ops:
  0.6 1.0 copy.43
  1.7 14.6 %all_gather.18 = bf16[32,4,16,128]{3,0,2,1:T(8,128)(2,1)S(1)} all-gather(bf16[8,4,16,128]{3,0,2,1:T(8,128)(2,1)S(1)} %copy.43), channel_id=1, replica_groups=mesh['gx'=8,'gy'=8,'af'=4] {'af'}, dimensions={0}, use_global_device_ids=true | all-gather | bytes 655360 | tf_op jit(solution)/shard_map/all_gather | solution.py:74
  16.3 1.3 collective-permute-start
  17.6 1.3 collective-permute-start.1
  19.9 15.3 %all_gather.22 = bf16[32,4,16,128]{3,0,2,1:T(8,128)(2,1)S(1)} all-gather(bf16[8,4,16,128]{3,0,2,1:T(8,128)(2,1)S(1)} %copy.46), channel_id=1, replica_groups=mesh['gx'=8,'gy'=8,'af'=4] {'af'}, dimensions={0}, use_global_device_ids=true | all-gather | bytes 655360 | tf_op jit(solution)/shard_map/all_gather | solution.py:74
  35.2 2.1 collective-permute-start.8
  37.4 1.3 collective-permute-start.9
  38.9 13.0 %all_gather.21 = bf16[32,32,3,3,3]{1,0,4,3,2:T(8,128)(2,1)S(1)} all-gather(bf16[8,32,3,3,3]{1,0,4,3,2:T(8,128)(2,1)S(1)} %copy-done.48), channel_id=1, replica_groups=mesh['gx'=8,'gy'=8,'af'=4] {'af'}, dimensions={0}, use_global_device_ids=true | all-gather | bytes 69120 | tf_op jit(solution)/shard_map/all_gather | solution.py:94
  52.3 13.0 %all_gather.20 = bf16[32,32,3,3,3]{1,0,4,3,2:T(8,128)(2,1)S(1)} all-gather(bf16[8,32,3,3,3]{1,0,4,3,2:T(8,128)(2,1)S(1)} %copy-done.50), channel_id=1, replica_groups=mesh['gx'=8,'gy'=8,'af'=4] {'af'}, dimensions={0}, use_global_device_ids=true | all-gather | bytes 69120 | tf_op jit(solution)/shard_map/all_gather | solution.py:93
  66.0 3.4 collective-permute-start.2
  69.4 1.3 collective-permute-start.3
  71.2 4.5 collective-permute-start.10
  75.8 1.5 collective-permute-start.11
  92.0 15.4 %all_gather.23 = bf16[32,4,16,128]{3,0,2,1:T(8,128)(2,1)S(1)} all-gather(bf16[8,4,16,128]{3,0,2,1:T(8,128)(2,1)S(1)} %get-tuple-element.51), channel_id=1, replica_groups=mesh['gx'=8,'gy'=8,'af'=4] {'af'}, dimensions={0}, use_global_device_ids=true | all-gather | bytes 655360 | tf_op jit(solution)/shard_map/all_gather | solution.py:74
  107.4 14.4 %all_gather.19 = bf16[32,4,16,128]{3,0,2,1:T(8,128)(2,1)S(1)} all-gather(bf16[8,4,16,128]{3,0,2,1:T(8,128)(2,1)S(1)} %get-tuple-element.48), channel_id=1, replica_groups=mesh['gx'=8,'gy'=8,'af'=4] {'af'}, dimensions={0}, use_global_device_ids=true | all-gather | bytes 655360 | tf_op jit(solution)/shard_map/all_gather | solution.py:74
  122.7 1.3 collective-permute-start.4
  123.9 1.5 collective-permute-start.5
  132.2 8.9 %collective-permute-start.12 = (bf16[32,1,16,128]{3,0,2,1:T(8,128)(2,1)S(1)}, bf16[32,1,16,128]{3,0,2,1:T(8,128)(2,1)S(1)}, u32[]{:S(2)}, u32[]{:S(2)}) collective-permute-start(bf16[32,1,16,128]{3,0,2,1:T(8,128)(2,1)S(1)} %get-tuple-element.27), channel_id=1, source_target_pairs={{0,32},{32,64},{64,96},{96,128},{128,160},{160,192},{192,224},{1,3... | collective-permute-start | bytes 393224 | tf_op jit(solution)/shard_map/ppermute | solution.py:16
  141.1 1.3 collective-permute-start.13
  144.3 4.4 collective-permute-start.6
  148.7 1.3 collective-permute-start.7
  150.2 9.7 %collective-permute-start.14 = (bf16[32,6,1,128]{3,0,2,1:T(8,128)(2,1)S(1)}, bf16[32,6,1,128]{3,0,2,1:T(8,128)(2,1)S(1)}, u32[]{:S(2)}, u32[]{:S(2)}) collective-permute-start(bf16[32,6,1,128]{3,0,2,1:T(8,128)(2,1)S(1)} %get-tuple-element.18), channel_id=1, source_target_pairs={{0,4},{4,8},{8,12},{12,16},{16,20},{20,24},{24,28},{1,5},{5,9},{9,... | collective-permute-start | bytes 147464 | tf_op jit(solution)/shard_map/ppermute | solution.py:16
  160.0 1.3 collective-permute-start.15
  164.8 7.0 %collective-permute-done.15 = bf16[32,6,1,128]{3,0,2,1:T(8,128)(2,1)S(1)} collective-permute-done((bf16[32,6,1,128]{3,0,2,1:T(8,128)(2,1)S(1)}, bf16[32,6,1,128]{3,0,2,1:T(8,128)(2,1)S(1)}, u32[]{:S(2)}, u32[]{:S(2)}) %collective-permute-start.15) | collective-permute-done | bytes 49184 | tf_op jit(solution)/shard_map/ppermute | solution.py:18
  173.7 1.0 fusion.228
  175.6 1.0 fusion.232
  177.5 1.0 fusion.236
  179.5 1.0 fusion.242
  181.4 1.0 fusion.209
  183.3 1.0 fusion.215
  185.3 1.0 fusion.221
  187.2 1.0 fusion.203
  190.3 1.0 fusion.310
  192.3 1.1 fusion.316
  194.2 1.0 fusion.322
  196.1 1.1 fusion.328
  198.1 1.1 convolution_bitcast_fusion.11
  200.0 1.0 convolution_bitcast_fusion.13
  201.1 1.0 convolution_bitcast_fusion.7
  203.0 1.1 convolution_bitcast_fusion.9
  213.4 413.0 %all-reduce.4 = (f32[8,32,3,3,3]{1,0,4,3,2:T(8,128)}, f32[8]{0:T(128)S(1)}, f32[8,32,3,3,3]{1,0,4,3,2:T(8,128)}) all-reduce(f32[8,32,3,3,3]{1,0,4,3,2:T(8,128)} %bitcast.1393, f32[8]{0:T(128)S(1)} %get-tuple-element.50, f32[8,32,3,3,3]{1,0,4,3,2:T(8,128)} %bitcast.1394), channel_id=1, replica_groups=mesh['gx'=8,'gy'=8,'af'=4] {'gx','gy'}, use_global_device_ids=true, to_apply=%region_0.1 | all-reduce | flops 13832 | bytes 110656 | tf_op jit(solution)/shard_map/psum | solution.py:108
  627.0 1.4 fusion.187
  628.3 1.2 fusion.181
  631.6 1.0 fusion.178
  634.5 1.1 fusion.108
  636.4 1.0 fusion.411
  640.3 1.0 fusion.391
  643.1 1.1 fusion.109
  (309 shorter events, 66.1 us)
Async XLA Ops:
  0.6 38.1 %copy-start.50 = (bf16[8,32,3,3,3]{1,0,4,3,2:T(8,128)(2,1)S(1)}, bf16[8,32,3,3,3]{1,0,4,3,2:T(8,128)(2,1)}, u32[]{:S(2)}) copy-start(bf16[8,32,3,3,3]{1,0,4,3,2:T(8,128)(2,1)} %param.6) | copy-start | bytes 41476
  1.7 37.2 %copy-start.48 = (bf16[8,32,3,3,3]{1,0,4,3,2:T(8,128)(2,1)S(1)}, bf16[8,32,3,3,3]{1,0,4,3,2:T(8,128)(2,1)}, u32[]{:S(2)}) copy-start(bf16[8,32,3,3,3]{1,0,4,3,2:T(8,128)(2,1)} %param.8) | copy-start | bytes 41476
  16.3 49.2 %collective-permute-start = (bf16[32,1,16,128]{3,0,2,1:T(8,128)(2,1)S(1)}, bf16[32,1,16,128]{3,0,2,1:T(8,128)(2,1)S(1)}, u32[]{:S(2)}, u32[]{:S(2)}) collective-permute-start(bf16[32,1,16,128]{3,0,2,1:T(8,128)(2,1)S(1)} %get-tuple-element.39), channel_id=1, source_target_pairs={{0,32},{32,64},{64,96},{96,128},{128,160},{160,192},{192,224},{1,3... | collective-permute-start | bytes 393224 | tf_op jit(solution)/shard_map/ppermute | solution.py:16
  17.6 48.3 %collective-permute-start.1 = (bf16[32,1,16,128]{3,0,2,1:T(8,128)(2,1)S(1)}, bf16[32,1,16,128]{3,0,2,1:T(8,128)(2,1)S(1)}, u32[]{:S(2)}, u32[]{:S(2)}) collective-permute-start(bf16[32,1,16,128]{3,0,2,1:T(8,128)(2,1)S(1)} %get-tuple-element.38), channel_id=1, source_target_pairs={{32,0},{64,32},{96,64},{128,96},{160,128},{192,160},{224,192},{33,... | collective-permute-start | bytes 393224 | tf_op jit(solution)/shard_map/ppermute | solution.py:18
  35.2 35.8 %collective-permute-start.8 = (bf16[32,1,16,128]{3,0,2,1:T(8,128)(2,1)S(1)}, bf16[32,1,16,128]{3,0,2,1:T(8,128)(2,1)S(1)}, u32[]{:S(2)}, u32[]{:S(2)}) collective-permute-start(bf16[32,1,16,128]{3,0,2,1:T(8,128)(2,1)S(1)} %get-tuple-element.29), channel_id=1, source_target_pairs={{0,32},{32,64},{64,96},{96,128},{128,160},{160,192},{192,224},{1,3... | collective-permute-start | bytes 393224 | tf_op jit(solution)/shard_map/ppermute | solution.py:16
  37.4 33.8 %collective-permute-start.9 = (bf16[32,1,16,128]{3,0,2,1:T(8,128)(2,1)S(1)}, bf16[32,1,16,128]{3,0,2,1:T(8,128)(2,1)S(1)}, u32[]{:S(2)}, u32[]{:S(2)}) collective-permute-start(bf16[32,1,16,128]{3,0,2,1:T(8,128)(2,1)S(1)} %get-tuple-element.28), channel_id=1, source_target_pairs={{32,0},{64,32},{96,64},{128,96},{160,128},{192,160},{224,192},{33,... | collective-permute-start | bytes 393224 | tf_op jit(solution)/shard_map/ppermute | solution.py:18
  65.5 121.7 %copy-start.47 = (bf16[8,32,3,3,3]{1,0,4,3,2:T(8,128)(2,1)}, bf16[8,32,3,3,3]{1,0,4,3,2:T(8,128)(2,1)S(1)}, u32[]{:S(2)}) copy-start(bf16[8,32,3,3,3]{1,0,4,3,2:T(8,128)(2,1)S(1)} %dynamic-slice_bitcast_fusion.1) | copy-start | bytes 41476
  66.0 11.6 %collective-permute-start.2 = (bf16[32,6,1,128]{3,0,2,1:T(8,128)(2,1)S(1)}, bf16[32,6,1,128]{3,0,2,1:T(8,128)(2,1)S(1)}, u32[]{:S(2)}, u32[]{:S(2)}) collective-permute-start(bf16[32,6,1,128]{3,0,2,1:T(8,128)(2,1)S(1)} %get-tuple-element.24), channel_id=1, source_target_pairs={{0,4},{4,8},{8,12},{12,16},{16,20},{20,24},{24,28},{1,5},{5,9},{9,... | collective-permute-start | bytes 147464 | tf_op jit(solution)/shard_map/ppermute | solution.py:16
  69.4 8.3 %collective-permute-start.3 = (bf16[32,6,1,128]{3,0,2,1:T(8,128)(2,1)S(1)}, bf16[32,6,1,128]{3,0,2,1:T(8,128)(2,1)S(1)}, u32[]{:S(2)}, u32[]{:S(2)}) collective-permute-start(bf16[32,6,1,128]{3,0,2,1:T(8,128)(2,1)S(1)} %get-tuple-element.25), channel_id=1, source_target_pairs={{4,0},{8,4},{12,8},{16,12},{20,16},{24,20},{28,24},{5,1},{9,5},{13... | collective-permute-start | bytes 147464 | tf_op jit(solution)/shard_map/ppermute | solution.py:18
  71.2 11.8 %collective-permute-start.10 = (bf16[32,6,1,128]{3,0,2,1:T(8,128)(2,1)S(1)}, bf16[32,6,1,128]{3,0,2,1:T(8,128)(2,1)S(1)}, u32[]{:S(2)}, u32[]{:S(2)}) collective-permute-start(bf16[32,6,1,128]{3,0,2,1:T(8,128)(2,1)S(1)} %get-tuple-element.20), channel_id=1, source_target_pairs={{0,4},{4,8},{8,12},{12,16},{16,20},{20,24},{24,28},{1,5},{5,9},{9,... | collective-permute-start | bytes 147464 | tf_op jit(solution)/shard_map/ppermute | solution.py:16
  75.8 7.3 %collective-permute-start.11 = (bf16[32,6,1,128]{3,0,2,1:T(8,128)(2,1)S(1)}, bf16[32,6,1,128]{3,0,2,1:T(8,128)(2,1)S(1)}, u32[]{:S(2)}, u32[]{:S(2)}) collective-permute-start(bf16[32,6,1,128]{3,0,2,1:T(8,128)(2,1)S(1)} %get-tuple-element.21), channel_id=1, source_target_pairs={{4,0},{8,4},{12,8},{16,12},{20,16},{24,20},{28,24},{5,1},{9,5},{13... | collective-permute-start | bytes 147464 | tf_op jit(solution)/shard_map/ppermute | solution.py:18
  122.7 21.2 %collective-permute-start.4 = (bf16[32,1,16,128]{3,0,2,1:T(8,128)(2,1)S(1)}, bf16[32,1,16,128]{3,0,2,1:T(8,128)(2,1)S(1)}, u32[]{:S(2)}, u32[]{:S(2)}) collective-permute-start(bf16[32,1,16,128]{3,0,2,1:T(8,128)(2,1)S(1)} %get-tuple-element.34), channel_id=1, source_target_pairs={{0,32},{32,64},{64,96},{96,128},{128,160},{160,192},{192,224},{1,3... | collective-permute-start | bytes 393224 | tf_op jit(solution)/shard_map/ppermute | solution.py:16
  123.9 20.3 %collective-permute-start.5 = (bf16[32,1,16,128]{3,0,2,1:T(8,128)(2,1)S(1)}, bf16[32,1,16,128]{3,0,2,1:T(8,128)(2,1)S(1)}, u32[]{:S(2)}, u32[]{:S(2)}) collective-permute-start(bf16[32,1,16,128]{3,0,2,1:T(8,128)(2,1)S(1)} %get-tuple-element.33), channel_id=1, source_target_pairs={{32,0},{64,32},{96,64},{128,96},{160,128},{192,160},{224,192},{33,... | collective-permute-start | bytes 393224 | tf_op jit(solution)/shard_map/ppermute | solution.py:18
  132.2 17.8 %collective-permute-start.12 = (bf16[32,1,16,128]{3,0,2,1:T(8,128)(2,1)S(1)}, bf16[32,1,16,128]{3,0,2,1:T(8,128)(2,1)S(1)}, u32[]{:S(2)}, u32[]{:S(2)}) collective-permute-start(bf16[32,1,16,128]{3,0,2,1:T(8,128)(2,1)S(1)} %get-tuple-element.27), channel_id=1, source_target_pairs={{0,32},{32,64},{64,96},{96,128},{128,160},{160,192},{192,224},{1,3... | collective-permute-start | bytes 393224 | tf_op jit(solution)/shard_map/ppermute | solution.py:16
  141.1 9.1 %collective-permute-start.13 = (bf16[32,1,16,128]{3,0,2,1:T(8,128)(2,1)S(1)}, bf16[32,1,16,128]{3,0,2,1:T(8,128)(2,1)S(1)}, u32[]{:S(2)}, u32[]{:S(2)}) collective-permute-start(bf16[32,1,16,128]{3,0,2,1:T(8,128)(2,1)S(1)} %get-tuple-element.26), channel_id=1, source_target_pairs={{32,0},{64,32},{96,64},{128,96},{160,128},{192,160},{224,192},{33,... | collective-permute-start | bytes 393224 | tf_op jit(solution)/shard_map/ppermute | solution.py:18
  143.8 6.3 copy-start.51
  144.3 67.9 %copy-start.3 = (bf16[32,6,16,128]{3,0,2,1:T(8,128)(2,1)}, bf16[32,6,16,128]{3,0,2,1:T(8,128)(2,1)S(1)}, u32[]{:S(2)}) copy-start(bf16[32,6,16,128]{3,0,2,1:T(8,128)(2,1)S(1)} %get-tuple-element.43) | copy-start | bytes 2359300
  144.3 43.9 %collective-permute-start.6 = (bf16[32,6,1,128]{3,0,2,1:T(8,128)(2,1)S(1)}, bf16[32,6,1,128]{3,0,2,1:T(8,128)(2,1)S(1)}, u32[]{:S(2)}, u32[]{:S(2)}) collective-permute-start(bf16[32,6,1,128]{3,0,2,1:T(8,128)(2,1)S(1)} %get-tuple-element.22), channel_id=1, source_target_pairs={{0,4},{4,8},{8,12},{12,16},{16,20},{20,24},{24,28},{1,5},{5,9},{9,... | collective-permute-start | bytes 147464 | tf_op jit(solution)/shard_map/ppermute | solution.py:16
  148.7 39.5 %collective-permute-start.7 = (bf16[32,6,1,128]{3,0,2,1:T(8,128)(2,1)S(1)}, bf16[32,6,1,128]{3,0,2,1:T(8,128)(2,1)S(1)}, u32[]{:S(2)}, u32[]{:S(2)}) collective-permute-start(bf16[32,6,1,128]{3,0,2,1:T(8,128)(2,1)S(1)} %get-tuple-element.23), channel_id=1, source_target_pairs={{4,0},{8,4},{12,8},{16,12},{20,16},{24,20},{28,24},{5,1},{9,5},{13... | collective-permute-start | bytes 147464 | tf_op jit(solution)/shard_map/ppermute | solution.py:18
  150.2 21.7 %copy-start = (bf16[32,6,16,128]{3,0,2,1:T(8,128)(2,1)}, bf16[32,6,16,128]{3,0,2,1:T(8,128)(2,1)S(1)}, u32[]{:S(2)}) copy-start(bf16[32,6,16,128]{3,0,2,1:T(8,128)(2,1)S(1)} %constant_dynamic-update-slice_fusion.17) | copy-start | bytes 2359300
  150.2 14.6 %collective-permute-start.14 = (bf16[32,6,1,128]{3,0,2,1:T(8,128)(2,1)S(1)}, bf16[32,6,1,128]{3,0,2,1:T(8,128)(2,1)S(1)}, u32[]{:S(2)}, u32[]{:S(2)}) collective-permute-start(bf16[32,6,1,128]{3,0,2,1:T(8,128)(2,1)S(1)} %get-tuple-element.18), channel_id=1, source_target_pairs={{0,4},{4,8},{8,12},{12,16},{16,20},{20,24},{24,28},{1,5},{5,9},{9,... | collective-permute-start | bytes 147464 | tf_op jit(solution)/shard_map/ppermute | solution.py:16
  160.0 11.9 %collective-permute-start.15 = (bf16[32,6,1,128]{3,0,2,1:T(8,128)(2,1)S(1)}, bf16[32,6,1,128]{3,0,2,1:T(8,128)(2,1)S(1)}, u32[]{:S(2)}, u32[]{:S(2)}) collective-permute-start(bf16[32,6,1,128]{3,0,2,1:T(8,128)(2,1)S(1)} %get-tuple-element.19), channel_id=1, source_target_pairs={{4,0},{8,4},{12,8},{16,12},{20,16},{24,20},{28,24},{5,1},{9,5},{13... | collective-permute-start | bytes 147464 | tf_op jit(solution)/shard_map/ppermute | solution.py:18
  164.8 9.9 %copy-start.43 = (bf16[32,6,1,128]{3,0,2,1:T(8,128)(2,1)}, bf16[32,6,1,128]{3,0,2,1:T(8,128)(2,1)S(1)}, u32[]{:S(2)}) copy-start(bf16[32,6,1,128]{3,0,2,1:T(8,128)(2,1)S(1)} %collective-permute-done.14) | copy-start | bytes 147460
  188.3 21.9 %copy-start.55 = (bf16[32,6,1,128]{3,0,2,1:T(8,128)(2,1)}, bf16[32,6,1,128]{3,0,2,1:T(8,128)(2,1)S(1)}, u32[]{:S(2)}) copy-start(bf16[32,6,1,128]{3,0,2,1:T(8,128)(2,1)S(1)} %collective-permute-done.6) | copy-start | bytes 147460
  188.3 23.9 %copy-start.57 = (bf16[32,6,1,128]{3,0,2,1:T(8,128)(2,1)}, bf16[32,6,1,128]{3,0,2,1:T(8,128)(2,1)S(1)}, u32[]{:S(2)}) copy-start(bf16[32,6,1,128]{3,0,2,1:T(8,128)(2,1)S(1)} %collective-permute-done.7) | copy-start | bytes 147460
  626.4 3.2 copy-start.1
  626.4 3.2 copy-start.44
  626.9 3.6 copy-start.24
  626.9 3.6 copy-start.34
  626.9 3.6 copy-start.35
  626.9 3.6 copy-start.36
  626.9 3.6 copy-start.37
  626.9 3.6 copy-start.38
  626.9 3.6 copy-start.39
  626.9 3.6 copy-start.40
  627.0 3.6 copy-start.41
  627.0 3.6 copy-start.42
  634.5 2.9 copy-start.58
  636.3 2.8 copy-start.23
  636.3 2.8 copy-start.25
  636.3 2.9 copy-start.26
  636.3 2.9 copy-start.27
  636.3 2.9 copy-start.28
  636.3 2.9 copy-start.29
  636.3 2.9 copy-start.30
  636.3 2.9 copy-start.31
  636.3 2.9 copy-start.32
  636.4 2.9 copy-start.33
  (28 other events, 66.5 us)
where the time goes:
time: 647 us; the launch traced here: 646 us
  blocking collectives  499 us (77%)
  matrix products  80.8 us (12%)
  starting transfers between devices  46.4 us (7%)
  waiting for transfers between devices  7.08 us (1%)
    psum x1, blocking collectives, body(): lax.psum((local_one, local_bias, local_two), ('gx', 'gy'))  413 us
    dot_general x108, matrix products, conv_valid(): jnp.einsum('oi,ixyz->oxyz', weight[:, :, off_x, off_y, off_z], window, pr...  65.3 us
    all_gather x4, blocking collectives, full_padded(): gathered = lax.all_gather(values, 'af', axis=0, tiled=True)  59.7 us
    ppermute x8, starting transfers between devices, with_halo(): lax.ppermute(tail, axis, [(i, (i + 1) % count) for i in range(ends)])  35.7 us
    dot_general x54, matrix products, kernel_grad(): jnp.einsum('oxyz,ixyz->oi', cot_field, window, preferred_element_type=jnp...  15.6 us
    all_gather x1, blocking collectives, body(): lax.all_gather(weight_one, 'af', axis=0, tiled=True)  13 us
    all_gather x1, blocking collectives, body(): lax.all_gather(weight_two, 'af', axis=0, tiled=True)  13 us
  transfers between devices with their start and end apart: 16, of which 1 were waited for; matrix products, arithmetic and copies ran while one was open for 6% of the time, Pallas kernels for 0%

commit v1 on v0

--- a/solution.py
+++ b/solution.py
@@ -3,6 +3,11 @@
 import jax.numpy as jnp
 from jax import lax
 from jax.sharding import PartitionSpec as P
+
+
+def by_each_axis(x, one, other):
+    inner = lax.psum(x, one)
+    return lax.psum(inner, other)
 
 
 def with_halo(cells, sides, width):
@@ -105,7 +110,9 @@
     local_one = kernel_grad(vol_pad, pre_grad)
     local_bias = jnp.sum(pre_grad, axis=(1, 2, 3), dtype=jnp.float32)
     input_grad = transposed(pre_grad, every_one).astype(jnp.bfloat16)
-    summed_one, summed_bias, summed_two = lax.psum((local_one, local_bias, local_two), ("gx", "gy"))
+    summed_one, summed_bias, summed_two = by_each_axis(
+        (local_one, local_bias, local_two), "gx", "gy"
+    )
     cell_total = (
         volume.shape[1]
         * lax.axis_size("gx")

time: 647 us -> 335 us (0.52)
  the two profiles are of different devices: /device:TPU:0 before, /device:TPU:4 now
where the time goes in v1:
time: 335 us; the launch traced here: 331 us
  blocking collectives  172 us (51%)
  matrix products  80.7 us (24%)
  starting transfers between devices  54.3 us (16%)
  waiting for transfers between devices  10.5 us (3%)
  local copies, waits for them, and re-layouts  5.88 us (2%)
  other arithmetic  4.83 us (1%)
    dot_general x108, matrix products, conv_valid(): jnp.einsum('oi,ixyz->oxyz', weight[:, :, off_x, off_y, off_z], window, pr...  65.2 us
    all_gather x4, blocking collectives, full_padded(): gathered = lax.all_gather(values, 'af', axis=0, tiled=True)  60.4 us
    psum x1, blocking collectives, by_each_axis(): return lax.psum(inner, other)  58 us
    ppermute x8, starting transfers between devices, with_halo(): lax.ppermute(tail, axis, [(i, (i + 1) % count) for i in range(ends)])  39.9 us
    psum x1, blocking collectives, by_each_axis(): inner = lax.psum(x, one)  28 us
    dot_general x54, matrix products, kernel_grad(): jnp.einsum('oxyz,ixyz->oi', cot_field, window, preferred_element_type=jnp...  15.5 us
    ppermute x8, starting transfers between devices, with_halo(): lax.ppermute(head, axis, [((i + 1) % count, i) for i in range(ends)])  14.4 us
    all_gather x1, blocking collectives, body(): lax.all_gather(weight_one, 'af', axis=0, tiled=True)  13 us
  transfers between devices with their start and end apart: 16, of which 2 were waited for; matrix products, arithmetic and copies ran while one was open for 11% of the time, Pallas kernels for 0%

profile of v1, /device:TPU:4, one launch (start us, length us, event | category | flops | bytes accessed | tf_op | source)
XLA Modules:
  0.0 330.8 jit_solution(6309157259139881229)
XLA Ops:
  0.6 1.0 copy.43
  1.7 16.4 %all_gather.18 = bf16[32,4,16,128]{3,0,2,1:T(8,128)(2,1)S(1)} all-gather(bf16[8,4,16,128]{3,0,2,1:T(8,128)(2,1)S(1)} %copy.43), channel_id=1, replica_groups=mesh['gx'=8,'gy'=8,'af'=4] {'af'}, dimensions={0}, use_global_device_ids=true | all-gather | bytes 655360 | tf_op jit(solution)/shard_map/all_gather | solution.py:79
  18.1 1.3 collective-permute-start
  19.4 1.3 collective-permute-start.1
  21.7 15.3 %all_gather.22 = bf16[32,4,16,128]{3,0,2,1:T(8,128)(2,1)S(1)} all-gather(bf16[8,4,16,128]{3,0,2,1:T(8,128)(2,1)S(1)} %copy.46), channel_id=1, replica_groups=mesh['gx'=8,'gy'=8,'af'=4] {'af'}, dimensions={0}, use_global_device_ids=true | all-gather | bytes 655360 | tf_op jit(solution)/shard_map/all_gather | solution.py:79
  37.0 2.1 collective-permute-start.8
  39.1 1.3 collective-permute-start.9
  40.6 13.0 %all_gather.21 = bf16[32,32,3,3,3]{1,0,4,3,2:T(8,128)(2,1)S(1)} all-gather(bf16[8,32,3,3,3]{1,0,4,3,2:T(8,128)(2,1)S(1)} %copy-done.48), channel_id=1, replica_groups=mesh['gx'=8,'gy'=8,'af'=4] {'af'}, dimensions={0}, use_global_device_ids=true | all-gather | bytes 69120 | tf_op jit(solution)/shard_map/all_gather | solution.py:99
  54.0 13.0 %all_gather.20 = bf16[32,32,3,3,3]{1,0,4,3,2:T(8,128)(2,1)S(1)} all-gather(bf16[8,32,3,3,3]{1,0,4,3,2:T(8,128)(2,1)S(1)} %copy-done.50), channel_id=1, replica_groups=mesh['gx'=8,'gy'=8,'af'=4] {'af'}, dimensions={0}, use_global_device_ids=true | all-gather | bytes 69120 | tf_op jit(solution)/shard_map/all_gather | solution.py:98
  67.7 3.1 collective-permute-start.2
  70.9 2.7 collective-permute-start.3
  74.1 6.8 %collective-permute-start.10 = (bf16[32,6,1,128]{3,0,2,1:T(8,128)(2,1)S(1)}, bf16[32,6,1,128]{3,0,2,1:T(8,128)(2,1)S(1)}, u32[]{:S(2)}, u32[]{:S(2)}) collective-permute-start(bf16[32,6,1,128]{3,0,2,1:T(8,128)(2,1)S(1)} %get-tuple-element.23), channel_id=1, source_target_pairs={{0,4},{4,8},{8,12},{12,16},{16,20},{20,24},{24,28},{1,5},{5,9},{9,... | collective-permute-start | bytes 147464 | tf_op jit(solution)/shard_map/ppermute | solution.py:21
  81.0 2.2 collective-permute-start.11
  88.9 4.0 %collective-permute-done.11 = bf16[32,6,1,128]{3,0,2,1:T(8,128)(2,1)S(1)} collective-permute-done((bf16[32,6,1,128]{3,0,2,1:T(8,128)(2,1)S(1)}, bf16[32,6,1,128]{3,0,2,1:T(8,128)(2,1)S(1)}, u32[]{:S(2)}, u32[]{:S(2)}) %collective-permute-start.11) | collective-permute-done | bytes 49184 | tf_op jit(solution)/shard_map/ppermute | solution.py:23
  101.9 14.2 %all_gather.23 = bf16[32,4,16,128]{3,0,2,1:T(8,128)(2,1)S(1)} all-gather(bf16[8,4,16,128]{3,0,2,1:T(8,128)(2,1)S(1)} %get-tuple-element.54), channel_id=1, replica_groups=mesh['gx'=8,'gy'=8,'af'=4] {'af'}, dimensions={0}, use_global_device_ids=true | all-gather | bytes 655360 | tf_op jit(solution)/shard_map/all_gather | solution.py:79
  116.1 14.5 %all_gather.19 = bf16[32,4,16,128]{3,0,2,1:T(8,128)(2,1)S(1)} all-gather(bf16[8,4,16,128]{3,0,2,1:T(8,128)(2,1)S(1)} %get-tuple-element.51), channel_id=1, replica_groups=mesh['gx'=8,'gy'=8,'af'=4] {'af'}, dimensions={0}, use_global_device_ids=true | all-gather | bytes 655360 | tf_op jit(solution)/shard_map/all_gather | solution.py:79
  131.5 1.3 collective-permute-start.4
  132.8 1.8 collective-permute-start.5
  141.3 8.5 %collective-permute-start.12 = (bf16[32,1,16,128]{3,0,2,1:T(8,128)(2,1)S(1)}, bf16[32,1,16,128]{3,0,2,1:T(8,128)(2,1)S(1)}, u32[]{:S(2)}, u32[]{:S(2)}) collective-permute-start(bf16[32,1,16,128]{3,0,2,1:T(8,128)(2,1)S(1)} %get-tuple-element.30), channel_id=1, source_target_pairs={{0,32},{32,64},{64,96},{96,128},{128,160},{160,192},{192,224},{1,3... | collective-permute-start | bytes 393224 | tf_op jit(solution)/shard_map/ppermute | solution.py:21
  149.8 1.3 collective-permute-start.13
  153.0 9.9 %collective-permute-start.6 = (bf16[32,6,1,128]{3,0,2,1:T(8,128)(2,1)S(1)}, bf16[32,6,1,128]{3,0,2,1:T(8,128)(2,1)S(1)}, u32[]{:S(2)}, u32[]{:S(2)}) collective-permute-start(bf16[32,6,1,128]{3,0,2,1:T(8,128)(2,1)S(1)} %get-tuple-element.25), channel_id=1, source_target_pairs={{0,4},{4,8},{8,12},{12,16},{16,20},{20,24},{24,28},{1,5},{5,9},{9,... | collective-permute-start | bytes 147464 | tf_op jit(solution)/shard_map/ppermute | solution.py:21
  162.9 1.9 collective-permute-start.7
  165.0 6.9 %collective-permute-start.14 = (bf16[32,6,1,128]{3,0,2,1:T(8,128)(2,1)S(1)}, bf16[32,6,1,128]{3,0,2,1:T(8,128)(2,1)S(1)}, u32[]{:S(2)}, u32[]{:S(2)}) collective-permute-start(bf16[32,6,1,128]{3,0,2,1:T(8,128)(2,1)S(1)} %get-tuple-element.21), channel_id=1, source_target_pairs={{0,4},{4,8},{8,12},{12,16},{16,20},{20,24},{24,28},{1,5},{5,9},{9,... | collective-permute-start | bytes 147464 | tf_op jit(solution)/shard_map/ppermute | solution.py:21
  171.9 1.9 collective-permute-start.15
  177.5 6.5 %collective-permute-done.15 = bf16[32,6,1,128]{3,0,2,1:T(8,128)(2,1)S(1)} collective-permute-done((bf16[32,6,1,128]{3,0,2,1:T(8,128)(2,1)S(1)}, bf16[32,6,1,128]{3,0,2,1:T(8,128)(2,1)S(1)}, u32[]{:S(2)}, u32[]{:S(2)}) %collective-permute-start.15) | collective-permute-done | bytes 49184 | tf_op jit(solution)/shard_map/ppermute | solution.py:23
  185.7 1.0 fusion.228
  187.7 1.0 fusion.232
  189.6 1.0 fusion.236
  191.5 1.0 fusion.242
  193.5 1.1 fusion.209
  195.4 1.0 fusion.215
  197.3 1.0 fusion.221
  199.2 1.0 fusion.203
  202.4 1.1 fusion.310
  204.3 1.0 fusion.316
  206.2 1.0 fusion.322
  208.1 1.1 fusion.328
  210.1 1.0 convolution_bitcast_fusion.11
  212.1 1.0 convolution_bitcast_fusion.13
  213.1 1.0 convolution_bitcast_fusion.7
  215.0 1.1 convolution_bitcast_fusion.9
  225.4 28.0 %all-reduce.5 = (f32[8,32,3,3,3]{1,0,4,3,2:T(8,128)}, f32[8]{0:T(128)S(1)}, f32[8,32,3,3,3]{1,0,4,3,2:T(8,128)}) all-reduce(f32[8,32,3,3,3]{1,0,4,3,2:T(8,128)} %bitcast.1393, f32[8]{0:T(128)S(1)} %get-tuple-element.53, f32[8,32,3,3,3]{1,0,4,3,2:T(8,128)} %bitcast.1394), channel_id=1, replica_groups=mesh['gx'=8,'gy'=8,'af'=4] {'gx'}, use_global_device_ids=true, to_apply=%region_0.1 | all-reduce | flops 13832 | bytes 110656 | tf_op jit(solution)/shard_map/psum | solution.py:9
  253.4 58.0 %all-reduce.4 = (f32[8,32,3,3,3]{1,0,4,3,2:T(8,128)}, f32[8]{0:T(128)S(1)}, f32[8,32,3,3,3]{1,0,4,3,2:T(8,128)}) all-reduce(f32[8,32,3,3,3]{1,0,4,3,2:T(8,128)} %get-tuple-element.18, f32[8]{0:T(128)S(1)} %get-tuple-element.19, f32[8,32,3,3,3]{1,0,4,3,2:T(8,128)} %get-tuple-element.20), channel_id=1, replica_groups=mesh['gx'=8,'gy'=8,'af'=4] {'gy'}, use_global_device_ids=true, to_apply=%region_1.2 | all-reduce | flops 13832 | bytes 110656 | tf_op jit(solution)/shard_map/psum | solution.py:10
  312.0 1.4 fusion.187
  313.3 1.2 fusion.181
  319.5 1.1 fusion.108
  321.4 1.0 fusion.411
  328.1 1.1 fusion.109
  (310 shorter events, 68.0 us)
Async XLA Ops:
  0.6 39.8 %copy-start.50 = (bf16[8,32,3,3,3]{1,0,4,3,2:T(8,128)(2,1)S(1)}, bf16[8,32,3,3,3]{1,0,4,3,2:T(8,128)(2,1)}, u32[]{:S(2)}) copy-start(bf16[8,32,3,3,3]{1,0,4,3,2:T(8,128)(2,1)} %param.6) | copy-start | bytes 41476
  1.7 39.0 %copy-start.48 = (bf16[8,32,3,3,3]{1,0,4,3,2:T(8,128)(2,1)S(1)}, bf16[8,32,3,3,3]{1,0,4,3,2:T(8,128)(2,1)}, u32[]{:S(2)}) copy-start(bf16[8,32,3,3,3]{1,0,4,3,2:T(8,128)(2,1)} %param.8) | copy-start | bytes 41476
  18.1 49.2 %collective-permute-start = (bf16[32,1,16,128]{3,0,2,1:T(8,128)(2,1)S(1)}, bf16[32,1,16,128]{3,0,2,1:T(8,128)(2,1)S(1)}, u32[]{:S(2)}, u32[]{:S(2)}) collective-permute-start(bf16[32,1,16,128]{3,0,2,1:T(8,128)(2,1)S(1)} %get-tuple-element.42), channel_id=1, source_target_pairs={{0,32},{32,64},{64,96},{96,128},{128,160},{160,192},{192,224},{1,3... | collective-permute-start | bytes 393224 | tf_op jit(solution)/shard_map/ppermute | solution.py:21
  19.4 48.3 %collective-permute-start.1 = (bf16[32,1,16,128]{3,0,2,1:T(8,128)(2,1)S(1)}, bf16[32,1,16,128]{3,0,2,1:T(8,128)(2,1)S(1)}, u32[]{:S(2)}, u32[]{:S(2)}) collective-permute-start(bf16[32,1,16,128]{3,0,2,1:T(8,128)(2,1)S(1)} %get-tuple-element.41), channel_id=1, source_target_pairs={{32,0},{64,32},{96,64},{128,96},{160,128},{192,160},{224,192},{33,... | collective-permute-start | bytes 393224 | tf_op jit(solution)/shard_map/ppermute | solution.py:23
  37.0 37.0 %collective-permute-start.8 = (bf16[32,1,16,128]{3,0,2,1:T(8,128)(2,1)S(1)}, bf16[32,1,16,128]{3,0,2,1:T(8,128)(2,1)S(1)}, u32[]{:S(2)}, u32[]{:S(2)}) collective-permute-start(bf16[32,1,16,128]{3,0,2,1:T(8,128)(2,1)S(1)} %get-tuple-element.32), channel_id=1, source_target_pairs={{0,32},{32,64},{64,96},{96,128},{128,160},{160,192},{192,224},{1,3... | collective-permute-start | bytes 393224 | tf_op jit(solution)/shard_map/ppermute | solution.py:21
  39.1 34.9 %collective-permute-start.9 = (bf16[32,1,16,128]{3,0,2,1:T(8,128)(2,1)S(1)}, bf16[32,1,16,128]{3,0,2,1:T(8,128)(2,1)S(1)}, u32[]{:S(2)}, u32[]{:S(2)}) collective-permute-start(bf16[32,1,16,128]{3,0,2,1:T(8,128)(2,1)S(1)} %get-tuple-element.31), channel_id=1, source_target_pairs={{32,0},{64,32},{96,64},{128,96},{160,128},{192,160},{224,192},{33,... | collective-permute-start | bytes 393224 | tf_op jit(solution)/shard_map/ppermute | solution.py:23
  67.3 132.0 %copy-start.47 = (bf16[8,32,3,3,3]{1,0,4,3,2:T(8,128)(2,1)}, bf16[8,32,3,3,3]{1,0,4,3,2:T(8,128)(2,1)S(1)}, u32[]{:S(2)}) copy-start(bf16[8,32,3,3,3]{1,0,4,3,2:T(8,128)(2,1)S(1)} %dynamic-slice_bitcast_fusion.1) | copy-start | bytes 41476
  67.7 15.8 %collective-permute-start.2 = (bf16[32,6,1,128]{3,0,2,1:T(8,128)(2,1)S(1)}, bf16[32,6,1,128]{3,0,2,1:T(8,128)(2,1)S(1)}, u32[]{:S(2)}, u32[]{:S(2)}) collective-permute-start(bf16[32,6,1,128]{3,0,2,1:T(8,128)(2,1)S(1)} %get-tuple-element.27), channel_id=1, source_target_pairs={{0,4},{4,8},{8,12},{12,16},{16,20},{20,24},{24,28},{1,5},{5,9},{9,... | collective-permute-start | bytes 147464 | tf_op jit(solution)/shard_map/ppermute | solution.py:21
  70.9 12.7 %collective-permute-start.3 = (bf16[32,6,1,128]{3,0,2,1:T(8,128)(2,1)S(1)}, bf16[32,6,1,128]{3,0,2,1:T(8,128)(2,1)S(1)}, u32[]{:S(2)}, u32[]{:S(2)}) collective-permute-start(bf16[32,6,1,128]{3,0,2,1:T(8,128)(2,1)S(1)} %get-tuple-element.28), channel_id=1, source_target_pairs={{4,0},{8,4},{12,8},{16,12},{20,16},{24,20},{28,24},{5,1},{9,5},{13... | collective-permute-start | bytes 147464 | tf_op jit(solution)/shard_map/ppermute | solution.py:23
  74.1 14.8 %collective-permute-start.10 = (bf16[32,6,1,128]{3,0,2,1:T(8,128)(2,1)S(1)}, bf16[32,6,1,128]{3,0,2,1:T(8,128)(2,1)S(1)}, u32[]{:S(2)}, u32[]{:S(2)}) collective-permute-start(bf16[32,6,1,128]{3,0,2,1:T(8,128)(2,1)S(1)} %get-tuple-element.23), channel_id=1, source_target_pairs={{0,4},{4,8},{8,12},{12,16},{16,20},{20,24},{24,28},{1,5},{5,9},{9,... | collective-permute-start | bytes 147464 | tf_op jit(solution)/shard_map/ppermute | solution.py:21
  81.0 12.0 %collective-permute-start.11 = (bf16[32,6,1,128]{3,0,2,1:T(8,128)(2,1)S(1)}, bf16[32,6,1,128]{3,0,2,1:T(8,128)(2,1)S(1)}, u32[]{:S(2)}, u32[]{:S(2)}) collective-permute-start(bf16[32,6,1,128]{3,0,2,1:T(8,128)(2,1)S(1)} %get-tuple-element.24), channel_id=1, source_target_pairs={{4,0},{8,4},{12,8},{16,12},{20,16},{24,20},{28,24},{5,1},{9,5},{13... | collective-permute-start | bytes 147464 | tf_op jit(solution)/shard_map/ppermute | solution.py:23
  131.5 21.0 %collective-permute-start.4 = (bf16[32,1,16,128]{3,0,2,1:T(8,128)(2,1)S(1)}, bf16[32,1,16,128]{3,0,2,1:T(8,128)(2,1)S(1)}, u32[]{:S(2)}, u32[]{:S(2)}) collective-permute-start(bf16[32,1,16,128]{3,0,2,1:T(8,128)(2,1)S(1)} %get-tuple-element.37), channel_id=1, source_target_pairs={{0,32},{32,64},{64,96},{96,128},{128,160},{160,192},{192,224},{1,3... | collective-permute-start | bytes 393224 | tf_op jit(solution)/shard_map/ppermute | solution.py:21
  132.8 20.1 %collective-permute-start.5 = (bf16[32,1,16,128]{3,0,2,1:T(8,128)(2,1)S(1)}, bf16[32,1,16,128]{3,0,2,1:T(8,128)(2,1)S(1)}, u32[]{:S(2)}, u32[]{:S(2)}) collective-permute-start(bf16[32,1,16,128]{3,0,2,1:T(8,128)(2,1)S(1)} %get-tuple-element.36), channel_id=1, source_target_pairs={{32,0},{64,32},{96,64},{128,96},{160,128},{192,160},{224,192},{33,... | collective-permute-start | bytes 393224 | tf_op jit(solution)/shard_map/ppermute | solution.py:23
  141.3 23.5 %collective-permute-start.12 = (bf16[32,1,16,128]{3,0,2,1:T(8,128)(2,1)S(1)}, bf16[32,1,16,128]{3,0,2,1:T(8,128)(2,1)S(1)}, u32[]{:S(2)}, u32[]{:S(2)}) collective-permute-start(bf16[32,1,16,128]{3,0,2,1:T(8,128)(2,1)S(1)} %get-tuple-element.30), channel_id=1, source_target_pairs={{0,32},{32,64},{64,96},{96,128},{128,160},{160,192},{192,224},{1,3... | collective-permute-start | bytes 393224 | tf_op jit(solution)/shard_map/ppermute | solution.py:21
  149.8 15.1 %collective-permute-start.13 = (bf16[32,1,16,128]{3,0,2,1:T(8,128)(2,1)S(1)}, bf16[32,1,16,128]{3,0,2,1:T(8,128)(2,1)S(1)}, u32[]{:S(2)}, u32[]{:S(2)}) collective-permute-start(bf16[32,1,16,128]{3,0,2,1:T(8,128)(2,1)S(1)} %get-tuple-element.29), channel_id=1, source_target_pairs={{32,0},{64,32},{96,64},{128,96},{160,128},{192,160},{224,192},{33,... | collective-permute-start | bytes 393224 | tf_op jit(solution)/shard_map/ppermute | solution.py:23
  152.5 12.4 %copy-start.51 = (f32[8,32,27]{1,0,2:T(8,128)}, f32[8,32,27]{1,0,2:T(8,128)S(1)}, u32[]{:S(2)}) copy-start(f32[8,32,27]{1,0,2:T(8,128)S(1)} %fusion.138) | copy-start | bytes 82948
  153.0 71.1 %copy-start.3 = (bf16[32,6,16,128]{3,0,2,1:T(8,128)(2,1)}, bf16[32,6,16,128]{3,0,2,1:T(8,128)(2,1)S(1)}, u32[]{:S(2)}) copy-start(bf16[32,6,16,128]{3,0,2,1:T(8,128)(2,1)S(1)} %get-tuple-element.46) | copy-start | bytes 2359300
  153.0 47.3 %collective-permute-start.6 = (bf16[32,6,1,128]{3,0,2,1:T(8,128)(2,1)S(1)}, bf16[32,6,1,128]{3,0,2,1:T(8,128)(2,1)S(1)}, u32[]{:S(2)}, u32[]{:S(2)}) collective-permute-start(bf16[32,6,1,128]{3,0,2,1:T(8,128)(2,1)S(1)} %get-tuple-element.25), channel_id=1, source_target_pairs={{0,4},{4,8},{8,12},{12,16},{16,20},{20,24},{24,28},{1,5},{5,9},{9,... | collective-permute-start | bytes 147464 | tf_op jit(solution)/shard_map/ppermute | solution.py:21
  162.9 37.4 %collective-permute-start.7 = (bf16[32,6,1,128]{3,0,2,1:T(8,128)(2,1)S(1)}, bf16[32,6,1,128]{3,0,2,1:T(8,128)(2,1)S(1)}, u32[]{:S(2)}, u32[]{:S(2)}) collective-permute-start(bf16[32,6,1,128]{3,0,2,1:T(8,128)(2,1)S(1)} %get-tuple-element.26), channel_id=1, source_target_pairs={{4,0},{8,4},{12,8},{16,12},{20,16},{24,20},{28,24},{5,1},{9,5},{13... | collective-permute-start | bytes 147464 | tf_op jit(solution)/shard_map/ppermute | solution.py:23
  165.0 19.0 %copy-start = (bf16[32,6,16,128]{3,0,2,1:T(8,128)(2,1)}, bf16[32,6,16,128]{3,0,2,1:T(8,128)(2,1)S(1)}, u32[]{:S(2)}) copy-start(bf16[32,6,16,128]{3,0,2,1:T(8,128)(2,1)S(1)} %constant_dynamic-update-slice_fusion.17) | copy-start | bytes 2359300
  165.0 12.5 %collective-permute-start.14 = (bf16[32,6,1,128]{3,0,2,1:T(8,128)(2,1)S(1)}, bf16[32,6,1,128]{3,0,2,1:T(8,128)(2,1)S(1)}, u32[]{:S(2)}, u32[]{:S(2)}) collective-permute-start(bf16[32,6,1,128]{3,0,2,1:T(8,128)(2,1)S(1)} %get-tuple-element.21), channel_id=1, source_target_pairs={{0,4},{4,8},{8,12},{12,16},{16,20},{20,24},{24,28},{1,5},{5,9},{9,... | collective-permute-start | bytes 147464 | tf_op jit(solution)/shard_map/ppermute | solution.py:21
  171.9 12.0 %collective-permute-start.15 = (bf16[32,6,1,128]{3,0,2,1:T(8,128)(2,1)S(1)}, bf16[32,6,1,128]{3,0,2,1:T(8,128)(2,1)S(1)}, u32[]{:S(2)}, u32[]{:S(2)}) collective-permute-start(bf16[32,6,1,128]{3,0,2,1:T(8,128)(2,1)S(1)} %get-tuple-element.22), channel_id=1, source_target_pairs={{4,0},{8,4},{12,8},{16,12},{20,16},{24,20},{28,24},{5,1},{9,5},{13... | collective-permute-start | bytes 147464 | tf_op jit(solution)/shard_map/ppermute | solution.py:23
  177.5 9.3 %copy-start.43 = (bf16[32,6,1,128]{3,0,2,1:T(8,128)(2,1)}, bf16[32,6,1,128]{3,0,2,1:T(8,128)(2,1)S(1)}, u32[]{:S(2)}) copy-start(bf16[32,6,1,128]{3,0,2,1:T(8,128)(2,1)S(1)} %collective-permute-done.14) | copy-start | bytes 147460
  183.9 2.9 copy-start.45
  200.3 21.9 %copy-start.55 = (bf16[32,6,1,128]{3,0,2,1:T(8,128)(2,1)}, bf16[32,6,1,128]{3,0,2,1:T(8,128)(2,1)S(1)}, u32[]{:S(2)}) copy-start(bf16[32,6,1,128]{3,0,2,1:T(8,128)(2,1)S(1)} %collective-permute-done.6) | copy-start | bytes 147460
  200.3 23.8 %copy-start.57 = (bf16[32,6,1,128]{3,0,2,1:T(8,128)(2,1)}, bf16[32,6,1,128]{3,0,2,1:T(8,128)(2,1)S(1)}, u32[]{:S(2)}) copy-start(bf16[32,6,1,128]{3,0,2,1:T(8,128)(2,1)S(1)} %collective-permute-done.7) | copy-start | bytes 147460
  311.4 3.2 copy-start.1
  311.4 3.2 copy-start.44
  311.9 3.6 %copy-start.24 = (f32[8,4,16,128]{3,0,2,1:T(8,128)S(1)}, f32[8,4,16,128]{3,0,2,1:T(8,128)}, u32[]{:S(2)}) copy-start(f32[8,4,16,128]{3,0,2,1:T(8,128)} %fusion.379) | copy-start | bytes 786436
  311.9 3.6 %copy-start.34 = (f32[8,4,16,128]{3,0,2,1:T(8,128)S(1)}, f32[8,4,16,128]{3,0,2,1:T(8,128)}, u32[]{:S(2)}) copy-start(f32[8,4,16,128]{3,0,2,1:T(8,128)} %fusion.238) | copy-start | bytes 786436
  311.9 3.6 %copy-start.35 = (f32[8,4,16,128]{3,0,2,1:T(8,128)S(1)}, f32[8,4,16,128]{3,0,2,1:T(8,128)}, u32[]{:S(2)}) copy-start(f32[8,4,16,128]{3,0,2,1:T(8,128)} %fusion.226) | copy-start | bytes 786436
  311.9 3.6 %copy-start.36 = (f32[8,4,16,128]{3,0,2,1:T(8,128)S(1)}, f32[8,4,16,128]{3,0,2,1:T(8,128)}, u32[]{:S(2)}) copy-start(f32[8,4,16,128]{3,0,2,1:T(8,128)} %fusion.228) | copy-start | bytes 786436
  311.9 3.6 %copy-start.37 = (f32[8,4,16,128]{3,0,2,1:T(8,128)S(1)}, f32[8,4,16,128]{3,0,2,1:T(8,128)}, u32[]{:S(2)}) copy-start(f32[8,4,16,128]{3,0,2,1:T(8,128)} %fusion.230) | copy-start | bytes 786436
  311.9 3.6 %copy-start.38 = (f32[8,4,16,128]{3,0,2,1:T(8,128)S(1)}, f32[8,4,16,128]{3,0,2,1:T(8,128)}, u32[]{:S(2)}) copy-start(f32[8,4,16,128]{3,0,2,1:T(8,128)} %fusion.232) | copy-start | bytes 786436
  311.9 3.6 %copy-start.39 = (f32[8,4,16,128]{3,0,2,1:T(8,128)S(1)}, f32[8,4,16,128]{3,0,2,1:T(8,128)}, u32[]{:S(2)}) copy-start(f32[8,4,16,128]{3,0,2,1:T(8,128)} %fusion.234) | copy-start | bytes 786436
  312.0 3.6 %copy-start.40 = (f32[8,4,16,128]{3,0,2,1:T(8,128)S(1)}, f32[8,4,16,128]{3,0,2,1:T(8,128)}, u32[]{:S(2)}) copy-start(f32[8,4,16,128]{3,0,2,1:T(8,128)} %fusion.236) | copy-start | bytes 786436
  312.0 3.6 %copy-start.41 = (f32[8,4,16,128]{3,0,2,1:T(8,128)S(1)}, f32[8,4,16,128]{3,0,2,1:T(8,128)}, u32[]{:S(2)}) copy-start(f32[8,4,16,128]{3,0,2,1:T(8,128)} %fusion.240) | copy-start | bytes 786436
  312.0 3.6 %copy-start.42 = (f32[8,4,16,128]{3,0,2,1:T(8,128)S(1)}, f32[8,4,16,128]{3,0,2,1:T(8,128)}, u32[]{:S(2)}) copy-start(f32[8,4,16,128]{3,0,2,1:T(8,128)} %fusion.242) | copy-start | bytes 786436
  319.5 2.9 copy-start.58
  321.3 2.8 copy-start.25
  321.3 2.8 copy-start.26
  321.3 2.8 copy-start.27
  321.3 2.8 copy-start.28
  321.3 2.8 copy-start.29
  321.3 2.8 copy-start.30
  321.3 2.8 copy-start.31
  321.4 2.8 copy-start.32
  321.4 2.8 copy-start.33
  (28 other events, 66.5 us)
